TPU v7x, 256 devices: a whole 4x4x8 slice. The times are simulated.
256 devices in a mesh: gx: 4 (over y), gy: 4 (over z_lo, core), gz: 16 (over z_hi, x).
Axes of the slice: x: 4, y: 4, z: 8 (z_hi: 4, z_lo: 2; z = z_hi * 2 + z_lo), core: 2. Of those that a mesh axis runs over, the one named last changes fastest.
Arguments:
- positions: float32 [4, 16, 16, 3, 128], P('gx', 'gy', 'gz'), may hold values from 0 to 1
- velocities: float32 [4, 16, 16, 3, 128], P('gx', 'gy', 'gz'), may hold values from -6 to 6
- charges: float32 [4, 16, 16, 128], P('gx', 'gy', 'gz'), may hold values from -3 to 3
- atom_types: int32 [4, 16, 16, 128], P('gx', 'gy', 'gz'), may hold values from 0 to 15
- atom_count: int32 [4, 16, 16], P('gx', 'gy', 'gz'), may hold values from 32 to 128
- sigma_type: float32 [16], replicated, may hold values from 0.15 to 0.35
- epsilon_type: float32 [16], replicated, may hold values from 0.3 to 3
- masses: float32 [4, 16, 16, 128], P('gx', 'gy', 'gz'), may hold values from 1 to 4
- pair_list: int32 [4, 4, 16, 2, 56], P('gx', 'gy', 'gz'), may hold values from 0 to 19, as said below
- pair_count: int32 [4, 4, 16], P('gx', 'gy', 'gz'), may hold values from 1 to 56, as said below
- pos_cotangent: float32 [4, 16, 16, 3, 128], P('gx', 'gy', 'gz'), may hold values from -6 to 6
- vel_cotangent: float32 [4, 16, 16, 3, 128], P('gx', 'gy', 'gz'), may hold values from -6 to 6
Outputs:
- pos_final: float32 [4, 16, 16, 3, 128], P('gx', 'gy', 'gz')
- vel_final: float32 [4, 16, 16, 3, 128], P('gx', 'gy', 'gz')
- grad_pos: float32 [4, 16, 16, 3, 128], P('gx', 'gy', 'gz')
- grad_vel: float32 [4, 16, 16, 3, 128], P('gx', 'gy', 'gz')
- grad_charge: float32 [4, 16, 16, 128], P('gx', 'gy', 'gz')
Inputs may be any that keep to these rules, and one draw needn't show every extreme that they name: `pair_list`: for k < pair_count[a, b, c] the two extended indices of slot k name blocks inside the global grid of 4 x 16 x 16 blocks, their coordinates differ by at most one in each dimension, and their smaller coordinate in each dimension lies in the device's own blocks; an unordered pair of blocks appears in at most one live slot over all devices. Slots at and past the count hold indices in range and are ignored. `pair_count`: some device has all 56 slots live in every draw.
All inputs are finite; a program needn't handle non-finite values.
Results may differ from a plain program's by a relative error of at most 0.00027.
Values sent between devices are 32-bit elements; how exact they have to be, the bound alone decides.
No kernel may reach another device: no remote copies, remote signals or barrier semaphores. Data moves between devices by JAX's collectives and lax.ppermute only.
A program may use at most 64 MiB of HBM per device.

v0:
```python
import functools

import jax
import jax.numpy as jnp
from jax import lax
from jax.experimental import pallas as pl
from jax.experimental.pallas import tpu as pltpu
from jax.sharding import PartitionSpec as P

STEPS = 5
SOFT = 0.04
KAPPA = 2.0
LOG2E = 1.4426950408889634
COULOMB = 4.0
TIME_STEP = 0.004
HALF = 0.5 * TIME_STEP
AXES = ("gx", "gy", "gz")
GRID = 16
OWN = 8
BLOCKS = 16
ROWS = 18
TILES = 2
GROUP = 8 * TILES
JOBS = 6
LIST = 56 * (128 // GROUP) + 16


def column_device(y, z):
    phys_y = y // 4
    phys_x = y % 4 if phys_y % 2 == 0 else 3 - y % 4
    phys_z = z // 2
    core = z % 2 if phys_z % 2 == 0 else 1 - z % 2
    return (phys_y * 4 + (phys_z % 2) * 2 + core) * 16 + (phys_z // 2) * 4 + phys_x


def column_of_device():
    gx, gy, gz = (lax.axis_index(name) for name in AXES)
    low, core = gy // 2, gy % 2
    high, phys_x = gz // 4, gz % 4
    phys_z = high * 2 + low
    y = gx * 4 + jnp.where(gx % 2 == 0, phys_x, 3 - phys_x)
    z = phys_z * 2 + jnp.where(phys_z % 2 == 0, core, 1 - core)
    return y, z


def spread_pairs(turn):
    return [
        ((a * 4 + b) * 16 + c, column_device(4 * b + (a + turn) % 4, c))
        for a in range(4)
        for b in range(4)
        for c in range(16)
    ]


def swap_pairs(axis, parity):
    pairs = []
    for y in range(GRID):
        for z in range(GRID):
            own = (y, z)[axis]
            other = own + 1 if own % 2 == parity else own - 1
            if 0 <= other < GRID:
                target = (other, z) if axis == 0 else (y, other)
                pairs.append((column_device(y, z), column_device(*target)))
    return pairs


def down_pairs(axis):
    pairs = []
    for y in range(GRID):
        for z in range(GRID):
            target = (y - 1, z) if axis == 0 else (y, z - 1)
            if min(target) >= 0:
                pairs.append((column_device(y, z), column_device(*target)))
    return pairs


def send(value, pairs):
    return lax.ppermute(value, AXES, pairs)


def list_kernel(list_ref, count_ref, place_ref, out_ref, total_ref):
    y_in_four, y_role, z_role = place_ref[0], place_ref[1], place_ref[2]
    total = jnp.int32(0)
    for a in range(4):

        count = jnp.minimum(list_ref[a, 112], 56)

        def one(k, total, a=a, count=count):
            def block(index):
                i = (index * 205) >> 11
                j = (index - 10 * i) >> 1
                return a + i, j, index & 1

            def number(x, j, l):
                return (((((j - y_in_four) & 1) ^ y_role) * 2 + (l ^ z_role)) * 4) + jnp.minimum(x, 3)

            first = block(list_ref[a, k])
            second = block(list_ref[a, 56 + k])
            mine = (jnp.minimum(first[1], second[1]) == y_in_four) & (k < count)
            one_number, two_number = number(*first), number(*second)
            one_count, two_count = count_ref[one_number], count_ref[two_number]
            swap = (first[2] > second[2]) | ((first[2] == second[2]) & (one_count > two_count))
            sign = jnp.where(swap, -1, 1)
            left = jnp.where(swap, two_number, one_number)
            right = jnp.where(swap, one_number, two_number)
            steps = (jnp.where(swap, two_count, one_count) + (GROUP - 1)) // GROUP
            own_left = ((left >> 3) << 2) + (left & 3)
            word = own_left + right * 16 + (jnp.where(left == right, 1, 2) << 18)
            for place in range(3):
                word = word + ((sign * (first[place] - second[place]) + 1) << (12 + 2 * place))
            for step in range(128 // GROUP):
                out_ref[total + step] = word + step * 256
            return total + jnp.where(mine, steps, 0)

        def four(k, total, one=one):
            for part in range(4):
                total = one(4 * k + part, total)
            return total

        total = lax.fori_loop(0, (count + 3) // 4, four, total)
    for job in range(JOBS):
        out_ref[total + job] = 0
    total_ref[0] = (total + JOBS - 1) // JOBS
    total_ref[1] = z_role


def inverse_of(value):
    guess = pl.reciprocal(value, approx=True)
    return guess * (2.0 - value * guess)


def sweep_tiles(mode, list_ref, total_ref, rows_ref, columns_refs, row_sum_ref, column_sum_ref):
    forces, pulled = "F" in mode, "J" in mode
    made = 3 * forces + 4 * pulled

    def one_job(word):
        left, right, step = word & 15, (word >> 4) & 15, (word >> 8) & 15
        offset = [(((word >> (12 + 2 * c)) & 3) - 1).astype(jnp.float32) for c in range(3)]
        weight = (word >> 18).astype(jnp.float32) * 0.5

        def row(c, scale=None, shift=None):
            value = rows_ref[c, pl.ds(right, 1), :]
            if scale is not None:
                value = value * scale
            if shift is not None:
                value = value - shift
            return jnp.broadcast_to(value, (8, 128))

        right_pos = [row(c, shift=offset[c]) for c in range(3)]
        right_charge = row(3, scale=8.0 * weight)
        right_half = row(4)
        right_depth = row(5, scale=24.0 * weight)
        right_cot = [row(6 + c) for c in range(3)] if pulled else None

        sums = None
        for tile in range(TILES):
            eight = pl.ds(pl.multiple_of(left * 128 + step * GROUP + 8 * tile, 8), 8)

            def column(c):
                return columns_refs[c // 3][c % 3, eight, :]

            d = [column(c) - right_pos[c] for c in range(3)]
            charge = column(3)
            half = column(4) + right_half
            depth = column(5) * right_depth
            s = d[0] * d[0] + d[1] * d[1] + d[2] * d[2]
            sigma2 = half * half
            r = inverse_of(s + sigma2)
            t = sigma2 * r
            p = t * t * t
            soft = s + SOFT
            ir = lax.rsqrt(soft)
            g = jnp.exp2((soft * ir) * (-KAPPA * LOG2E)) * ir
            fade = jnp.maximum(1.0 - s, 0.0)
            fade2 = fade * fade
            fr = fade * r
            ir2 = ir * ir
            fade_kappa = fade * (ir + 0.5 * ir2)
            fade2h = fade2 * (g * (3.0 + fade_kappa))
            dp = depth * p
            charges = charge * right_charge
            A = (fade2 * dp) * ((p - 1.0) + fr * (2.0 * p - 1.0)) + charges * fade2h
            values = []
            if forces:
                values += [A * d[c] for c in range(3)]
            if pulled:
                w = [column(6 + c) - right_cot[c] for c in range(3)]
                dw = d[0] * w[0] + d[1] * w[1] + d[2] * w[2]
                lj = (2.0 * p - 2.0) + fr * ((12.0 * p - 6.0) + fr * (14.0 * p - 4.0))
                m2 = ir2 * (1.0 + 1.5 * ir + 0.75 * ir2)
                coulomb = 6.0 * (1.0 + fade_kappa) + fade2 * m2
                B = (-2.0 * fade) * (dp * lj + (charges * g) * coulomb) * dw
                values += [A * w[c] + B * d[c] for c in range(3)]
                common = fade2h * dw
                values += [common * right_charge]
                last = common * charge
            for place, value in enumerate(values):
                row_sum_ref[place, eight, :] = row_sum_ref[place, eight, :] + value
            if pulled:
                values[-1] = -last
            sums = values if sums is None else [a + b for a, b in zip(sums, values)]
        if pulled:
            sums[-1] = sums[-1] * (8.0 * weight)
        for place in range(made):
            column_sum_ref[place, right] = column_sum_ref[place, right] + sums[place]

    def one_step(k, carry):
        for job in range(JOBS):
            one_job(list_ref[k * JOBS + job])
        return carry

    lax.fori_loop(0, total_ref[0], one_step, jnp.int32(0))


def sweep_kernel(mode, first, kick, list_ref, total_ref, *refs):
    forces, pulled = "F" in mode, "J" in mode
    made = 3 * forces + 4 * pulled
    names = ["ext"] + (["params"] if not first or mode == "J" else []) + (["places"] if mode == "J" else [])
    if mode != "J":
        names += ["x", "v"] if not first else []
        names += [] if first else ["C", "rC", "D", "rD"]
    else:
        names += ["x", "ax", "av", "C", "rC", "D", "rD", "charge"] + (["v"] if first else [])
    outs = ["A", "B"] + (["places"] if mode != "J" else []) + (["params"] if mode == "F" and first else [])
    if mode == "F" and not first:
        outs += ["x_out", "v_out"]
    if mode == "FJ":
        outs += ["x_out", "v_out", "charge_out"]
    if mode == "J":
        outs += ["ax_out", "av_out", "charge_out"] + (["v_out"] if first else [])
    scratch = ["rows", "cotangents", "row_sum", "column_sum"]
    r = dict(zip(names + outs + scratch, refs))
    ext = r["ext"]
    inverse = ext[9]

    def received(c):
        return jnp.concatenate([r["C"][c] + r["rC"][c], r["D"][c] + r["rD"][c]], axis=0)

    position, cotangent = [], []
    for c in range(3):
        if mode != "J":
            if first:
                position.append(ext[c])
            else:
                velocity = r["v"][c] + kick * inverse * received(c)
                position.append(r["x"][c] + TIME_STEP * velocity)
                r["x_out"][c] = position[c]
                r["v_out"][c] = velocity
            if pulled:
                cotangent.append(HALF * inverse * ext[13 + c])
        else:
            if first:
                r["v_out"][c] = r["v"][c] + HALF * inverse * received(c)
            ax = r["ax"][c] + received(c + 3 if first else c)
            av = r["av"][c] + TIME_STEP * ax
            r["ax_out"][c] = ax
            r["av_out"][c] = av
            position.append(r["x"][c])
            cotangent.append(kick * inverse * av)
    _spread_and_sweep(mode, first, ext, position, cotangent, list_ref, total_ref, r, made, pulled)


def _spread_and_sweep(mode, first, ext, position, cotangent, list_ref, total_ref, r, made, pulled):
    rows = r["rows"]
    own_first = total_ref[1] == 0
    quantities = position + [ext[6], 0.5 * ext[7], ext[8]] + cotangent
    for place, value in enumerate(quantities):
        rows[place] = value
        fresh = (mode != "J", mode == "F" and first, True)[place // 3]
        if not fresh:
            continue
        target = (r["places"], r.get("params"), r["cotangents"])[place // 3]
        near = jnp.concatenate([value[0:4], value[8:12]], axis=0)
        far = jnp.concatenate([value[4:8], value[12:16]], axis=0)
        turned = jnp.where(own_first, near, far).T
        for e in range(OWN):
            target[place % 3, e * 128 : (e + 1) * 128, :] = jnp.broadcast_to(turned[:, e : e + 1], (128, 128))
    r["row_sum"][...] = jnp.zeros(r["row_sum"].shape, jnp.float32)
    r["column_sum"][...] = jnp.zeros(r["column_sum"].shape, jnp.float32)
    sweep_tiles(mode, list_ref, total_ref, rows, (r["places"], r["params"], r["cotangents"]), r["row_sum"], r["column_sum"])
    lane = lax.broadcasted_iota(jnp.int32, (128, OWN), 1)
    for c in range(made):
        by_atom = jnp.zeros((128, OWN), jnp.float32)
        for e in range(OWN):
            total = jnp.sum(r["row_sum"][c, e * 128 : (e + 1) * 128, :], axis=1, keepdims=True)
            by_atom = jnp.where(lane == e, jnp.broadcast_to(total, (128, OWN)), by_atom)
        own = by_atom.T
        others = jnp.sum(r["column_sum"][c], axis=1)
        A = jnp.where(own_first, own, 0.0) - jnp.concatenate([others[0:4], others[8:12]], axis=0)
        B = jnp.where(own_first, 0.0, own) - jnp.concatenate([others[4:8], others[12:16]], axis=0)
        if pulled and c == made - 1:
            total = jnp.concatenate([A[0:4], B[0:4], A[4:8], B[4:8]], axis=0)
            if mode == "J":
                total = total + r["charge"][...]
            r["charge_out"][...] = total
        else:
            r["A"][c] = A
            r["B"][c] = B


def sweep(mode, first, kick, plist, total, arrays):
    forces, pulled = "F" in mode, "J" in mode
    sent = 3 * forces + 3 * pulled
    made = 3 * forces + 4 * pulled
    quantities = 6 + 3 * pulled
    f32 = jnp.float32
    exchange = jax.ShapeDtypeStruct((sent, 8, 128), f32)
    vector = jax.ShapeDtypeStruct((3, BLOCKS, 128), f32)
    scalar = jax.ShapeDtypeStruct((BLOCKS, 128), f32)
    wide = jax.ShapeDtypeStruct((3, OWN * 128, 128), f32)
    outs = [exchange, exchange] + ([wide] if mode != "J" else []) + ([wide] if mode == "F" and first else [])
    if mode == "F" and not first:
        outs += [vector, vector]
    if mode == "FJ":
        outs += [vector, vector, scalar]
    if mode == "J":
        outs += [vector, vector, scalar] + ([vector] if first else [])
    vmem = pl.BlockSpec(memory_space=pltpu.VMEM)
    smem = pl.BlockSpec(memory_space=pltpu.SMEM)
    return pl.pallas_call(
        functools.partial(sweep_kernel, mode, first, kick),
        out_shape=outs,
        in_specs=[smem, smem] + [vmem] * len(arrays),
        out_specs=[vmem] * len(outs),
        scratch_shapes=[
            pltpu.VMEM((quantities, BLOCKS, 128), f32),
            pltpu.VMEM((3, OWN * 128 if pulled else 8, 128), f32),
            pltpu.VMEM((made, OWN * 128, 128), f32),
            pltpu.VMEM((made, BLOCKS, 8, 128), f32),
        ],
        compiler_params=pltpu.CompilerParams(vmem_limit_bytes=32 * 1024 * 1024),
        name=f"sweep_{mode}",
    )(plist, total, *arrays)


def exchanged(A, B):
    rA, rB = send(A, swap_pairs(1, 0)), send(B, swap_pairs(1, 1))
    T0, T1 = A + rA, B + rB
    C = jnp.concatenate([T0[:, 0:4], T1[:, 0:4]], axis=1)
    D = jnp.concatenate([T0[:, 4:8], T1[:, 4:8]], axis=1)
    return C, send(C, swap_pairs(0, 0)), D, send(D, swap_pairs(0, 1))


def on_device(
    positions,
    velocities,
    charges,
    atom_types,
    atom_count,
    sigma_type,
    epsilon_type,
    masses,
    pair_list,
    pair_count,
    pos_cotangent,
    vel_cotangent,
):
    f32 = jnp.float32
    a = lax.axis_index("gx")
    y, z = column_of_device()
    y_even, z_even = y % 2 == 0, z % 2 == 0
    counts = atom_count[0, :, 0]
    alive = (lax.broadcasted_iota(jnp.int32, (4, 128), 1) < counts[:, None]).astype(f32)
    kinds = (atom_types[0, :, 0][:, None, :] == lax.broadcasted_iota(jnp.int32, (16, 1), 0)).astype(f32)
    sigma = jnp.sum(kinds * sigma_type[:, None], axis=1)
    epsilon = jnp.sum(kinds * epsilon_type[:, None], axis=1)
    listed = jnp.concatenate(
        [pair_list[0, 0, 0].reshape(112), jnp.broadcast_to(pair_count[0, 0, 0], (16,))]
    ).astype(f32)
    bundle = jnp.concatenate(
        [
            positions[0, :, 0],
            velocities[0, :, 0],
            jnp.stack(
                [charges[0, :, 0] * alive, sigma, jnp.sqrt(epsilon) * alive, 1.0 / masses[0, :, 0]], axis=1
            ),
            pos_cotangent[0, :, 0],
            vel_cotangent[0, :, 0],
            jnp.broadcast_to(counts.astype(f32)[:, None, None], (4, 1, 128)),
            jnp.broadcast_to(listed[None, None, :], (4, 1, 128)),
        ],
        axis=1,
    )
    turned = lax.dynamic_slice_in_dim(jnp.concatenate([bundle, bundle]), a, 4)
    got = [send(turned[t], spread_pairs(t)) for t in range(4)]
    stacked = jnp.stack(got[::-1])
    y_in_four = y % 4
    own = lax.dynamic_slice_in_dim(jnp.concatenate([stacked, stacked]), 3 - y_in_four, 4)
    own = jnp.swapaxes(own, 0, 1)
    lists = own[17].astype(jnp.int32)
    own = own[:17]
    upper = send(own, down_pairs(1))
    wide = jnp.where(
        z_even, jnp.concatenate([upper, own], axis=1), jnp.concatenate([own, upper], axis=1)
    )
    upper = send(wide, down_pairs(0))
    ext = jnp.where(
        y_even, jnp.concatenate([upper, wide], axis=1), jnp.concatenate([wide, upper], axis=1)
    )
    y_role, z_role = jnp.where(y_even, 1, 0), jnp.where(z_even, 1, 0)
    smem = pl.BlockSpec(memory_space=pltpu.SMEM)
    plist, total = pl.pallas_call(
        list_kernel,
        out_shape=[jax.ShapeDtypeStruct((LIST,), jnp.int32), jax.ShapeDtypeStruct((2,), jnp.int32)],
        in_specs=[smem] * 3,
        out_specs=[smem] * 2,
        name="keep_pairs",
    )(
        lists,
        ext[16, :, 0].astype(jnp.int32),
        jnp.stack([y_in_four, y_role, z_role]).astype(jnp.int32),
    )
    A, B, places, params = sweep("F", True, 0.0, plist, total, [ext])
    history = [(ext[0:3], places)]
    x, v = ext[0:3], ext[3:6]
    for step in range(STEPS):
        parts = exchanged(A, B)
        kick = HALF if step == 0 else TIME_STEP
        mode = "F" if step < STEPS - 1 else "FJ"
        A, B, places, x, v, *rest = sweep(mode, False, kick, plist, total, [ext, params, x, v, *parts])
        history.append((x, places))
    charge = rest[0]
    ax, av = ext[10:13], ext[13:16]
    for step in range(STEPS - 1, -1, -1):
        parts = exchanged(A, B)
        first = step == STEPS - 1
        factor = TIME_STEP if step > 0 else HALF
        A, B, ax, av, charge, *rest = sweep(
            "J",
            first,
            factor,
            plist,
            total,
            [ext, params, history[step][1], history[step][0], ax, av, *parts, charge] + ([v] if first else []),
        )
        if first:
            v = rest[0]
    sides = charge.reshape(2, 2, 4, 128)
    A = jnp.concatenate([A, sides[:, 0].reshape(1, 8, 128)])
    B = jnp.concatenate([B, sides[:, 1].reshape(1, 8, 128)])
    C, rC, D, rD = exchanged(A, B)
    sums = jnp.concatenate([C + rC, D + rD], axis=1)
    whole = jnp.concatenate([x, v, ax + sums[:3], av, sums[3:4]])
    mine = lax.dynamic_slice_in_dim(whole, (y_role * 2 + z_role) * 4, 4, axis=1)
    mine = jnp.swapaxes(mine, 0, 1)
    turned = lax.dynamic_slice_in_dim(jnp.concatenate([mine, mine]), (y_in_four + 1) % 4, 4)
    got = [send(turned[3 - t], [(q, p) for p, q in spread_pairs(t)]) for t in range(4)]
    stacked = jnp.stack(got)
    out = lax.dynamic_slice_in_dim(jnp.concatenate([stacked, stacked]), (4 - a) % 4, 4)
    out = out[None, :, None]
    return (
        out[:, :, :, 0:3],
        out[:, :, :, 3:6],
        out[:, :, :, 6:9],
        out[:, :, :, 9:12],
        out[:, :, :, 12] * alive[None, :, None],
    )


def solution(mesh):
    vector = P("gx", "gy", "gz", None, None)
    scalar = P("gx", "gy", "gz", None)
    block = P("gx", "gy", "gz")
    in_specs = (
        vector, vector, scalar, scalar, block, P(), P(), scalar, vector, block, vector, vector,
    )
    out_specs = (vector, vector, vector, vector, scalar)
    return jax.shard_map(on_device, mesh=mesh, in_specs=in_specs, out_specs=out_specs, check_vma=False)
```

profile of v0, /device:TPU:96, one launch (start us, length us, event | category | flops | bytes accessed | tf_op | source)
XLA Modules:
  0.0 312.4 jit_solution(2001561723397219288)
XLA Ops:
  6.6 5.6 %collective-permute-start.2 = (f32[18,128]{1,0:T(8,128)S(1)}, f32[18,128]{1,0:T(8,128)S(1)}, u32[]{:S(2)}, u32[]{:S(2)}) collective-permute-start(f32[18,128]{1,0:T(8,128)S(1)} %get-tuple-element.141), channel_id=1, source_target_pairs={{0,1},{1,17},{2,49},{3,33},{4,5},{5,21},{6,53},{7,37},{8,9},{9,25}... | collective-permute-start | bytes 27656 | tf_op jit(solution)/shard_map/ppermute | solution.py:78
  12.2 5.2 %collective-permute-start.1 = (f32[18,128]{1,0:T(8,128)S(1)}, f32[18,128]{1,0:T(8,128)S(1)}, u32[]{:S(2)}, u32[]{:S(2)}) collective-permute-start(f32[18,128]{1,0:T(8,128)S(1)} %get-tuple-element.142), channel_id=1, source_target_pairs={{0,2},{1,18},{2,50},{3,34},{4,6},{5,22},{6,54},{7,38},{8,10},{9,26... | collective-permute-start | bytes 27656 | tf_op jit(solution)/shard_map/ppermute | solution.py:78
  31.1 4.5 %collective-permute-done.4 = f32[17,4,128]{2,1,0:T(4,128)S(1)} collective-permute-done((f32[17,4,128]{2,1,0:T(4,128)S(1)}, f32[17,4,128]{2,1,0:T(4,128)S(1)}, u32[]{:S(2)}, u32[]{:S(2)}) %collective-permute-start.4) | collective-permute-done | bytes 34848 | tf_op jit(solution)/shard_map/ppermute | solution.py:78
  66.1 6.0 %collective-permute-start.11 = (f32[3,8,128]{2,1,0:T(8,128)S(1)}, f32[3,8,128]{2,1,0:T(8,128)S(1)}, u32[]{:S(2)}, u32[]{:S(2)}) collective-permute-start(f32[3,8,128]{2,1,0:T(8,128)S(1)} %get-tuple-element.70), channel_id=1, source_target_pairs={{16,48},{48,16},{32,4},{4,32},{20,52},{52,20},{36,8},{8,36},{24,56... | collective-permute-start | bytes 36872 | tf_op jit(solution)/shard_map/ppermute | solution.py:78
  83.0 5.6 %collective-permute-start.15 = (f32[3,8,128]{2,1,0:T(8,128)S(1)}, f32[3,8,128]{2,1,0:T(8,128)S(1)}, u32[]{:S(2)}, u32[]{:S(2)}) collective-permute-start(f32[3,8,128]{2,1,0:T(8,128)S(1)} %get-tuple-element.74), channel_id=1, source_target_pairs={{16,48},{48,16},{32,4},{4,32},{20,52},{52,20},{36,8},{8,36},{24,56... | collective-permute-start | bytes 36872 | tf_op jit(solution)/shard_map/ppermute | solution.py:78
  100.6 4.4 %collective-permute-start.19 = (f32[3,8,128]{2,1,0:T(8,128)S(1)}, f32[3,8,128]{2,1,0:T(8,128)S(1)}, u32[]{:S(2)}, u32[]{:S(2)}) collective-permute-start(f32[3,8,128]{2,1,0:T(8,128)S(1)} %get-tuple-element.78), channel_id=1, source_target_pairs={{16,48},{48,16},{32,4},{4,32},{20,52},{52,20},{36,8},{8,36},{24,56... | collective-permute-start | bytes 36872 | tf_op jit(solution)/shard_map/ppermute | solution.py:78
  107.4 5.5 %collective-permute-start.20 = (f32[3,8,128]{2,1,0:T(8,128)S(1)}, f32[3,8,128]{2,1,0:T(8,128)S(1)}, u32[]{:S(2)}, u32[]{:S(2)}) collective-permute-start(f32[3,8,128]{2,1,0:T(8,128)S(1)} %pad_maximum_fusion.12.refs_4_), channel_id=1, source_target_pairs={{0,1},{16,17},{48,49},{32,33},{4,5},{20,21},{52,53},{36,37},{8,9},... | collective-permute-start | bytes 36872 | tf_op jit(solution)/shard_map/ppermute | solution.py:78
  121.6 4.4 %collective-permute-done.23 = f32[3,8,128]{2,1,0:T(8,128)S(1)} collective-permute-done((f32[3,8,128]{2,1,0:T(8,128)S(1)}, f32[3,8,128]{2,1,0:T(8,128)S(1)}, u32[]{:S(2)}, u32[]{:S(2)}) %collective-permute-start.23) | collective-permute-done | bytes 12320 | tf_op jit(solution)/shard_map/ppermute | solution.py:78
  126.0 4.9 %collective-permute-start.24 = (f32[3,8,128]{2,1,0:T(8,128)S(1)}, f32[3,8,128]{2,1,0:T(8,128)S(1)}, u32[]{:S(2)}, u32[]{:S(2)}) collective-permute-start(f32[3,8,128]{2,1,0:T(8,128)S(1)} %pad_maximum_fusion.14.refs_4_), channel_id=1, source_target_pairs={{0,1},{16,17},{48,49},{32,33},{4,5},{20,21},{52,53},{36,37},{8,9},... | collective-permute-start | bytes 36872 | tf_op jit(solution)/shard_map/ppermute | solution.py:78
  132.5 5.2 %sweep_FJ.1 = (f32[6,8,128]{2,1,0:T(8,128)S(1)}, f32[6,8,128]{2,1,0:T(8,128)S(1)}, f32[3,1024,128]{2,1,0:T(8,128)}, f32[3,16,128]{2,1,0:T(8,128)S(1)}, f32[3,16,128]{2,1,0:T(8,128)S(1)}, /*index=5*/f32[16,128]{1,0:T(8,128)S(1)}) custom-call(s32[464]{0:T(512)S(1)} %copy-done.2, s32[2]{0:T(128)S(1)} %copy-done.4, ...), custom_call_target="tpu_custom_call" | custom-call | tf_op jit(solution)/shard_map/sweep_FJ/pallas_call | solution.py:320
  140.8 4.7 %collective-permute-done.27 = f32[6,8,128]{2,1,0:T(8,128)S(1)} collective-permute-done((f32[6,8,128]{2,1,0:T(8,128)S(1)}, f32[6,8,128]{2,1,0:T(8,128)S(1)}, u32[]{:S(2)}, u32[]{:S(2)}) %collective-permute-start.27) | collective-permute-done | bytes 24608 | tf_op jit(solution)/shard_map/ppermute | solution.py:78
  145.5 6.9 %collective-permute-start.28 = (f32[6,8,128]{2,1,0:T(8,128)S(1)}, f32[6,8,128]{2,1,0:T(8,128)S(1)}, u32[]{:S(2)}, u32[]{:S(2)}) collective-permute-start(f32[6,8,128]{2,1,0:T(8,128)S(1)} %pad_maximum_fusion.refs_6_), channel_id=1, source_target_pairs={{0,1},{16,17},{48,49},{32,33},{4,5},{20,21},{52,53},{36,37},{8,9},... | collective-permute-start | bytes 73736 | tf_op jit(solution)/shard_map/ppermute | solution.py:78
  162.7 4.8 %collective-permute-done.31 = f32[3,8,128]{2,1,0:T(8,128)S(1)} collective-permute-done((f32[3,8,128]{2,1,0:T(8,128)S(1)}, f32[3,8,128]{2,1,0:T(8,128)S(1)}, u32[]{:S(2)}, u32[]{:S(2)}) %collective-permute-start.31) | collective-permute-done | bytes 12320 | tf_op jit(solution)/shard_map/ppermute | solution.py:78
  167.6 4.9 %collective-permute-start.32 = (f32[3,8,128]{2,1,0:T(8,128)S(1)}, f32[3,8,128]{2,1,0:T(8,128)S(1)}, u32[]{:S(2)}, u32[]{:S(2)}) collective-permute-start(f32[3,8,128]{2,1,0:T(8,128)S(1)} %pad_maximum_fusion.16.refs_6_), channel_id=1, source_target_pairs={{0,1},{16,17},{48,49},{32,33},{4,5},{20,21},{52,53},{36,37},{8,9},... | collective-permute-start | bytes 36872 | tf_op jit(solution)/shard_map/ppermute | solution.py:78
  183.1 4.8 %collective-permute-done.35 = f32[3,8,128]{2,1,0:T(8,128)S(1)} collective-permute-done((f32[3,8,128]{2,1,0:T(8,128)S(1)}, f32[3,8,128]{2,1,0:T(8,128)S(1)}, u32[]{:S(2)}, u32[]{:S(2)}) %collective-permute-start.35) | collective-permute-done | bytes 12320 | tf_op jit(solution)/shard_map/ppermute | solution.py:78
  187.9 5.3 %collective-permute-start.36 = (f32[3,8,128]{2,1,0:T(8,128)S(1)}, f32[3,8,128]{2,1,0:T(8,128)S(1)}, u32[]{:S(2)}, u32[]{:S(2)}) collective-permute-start(f32[3,8,128]{2,1,0:T(8,128)S(1)} %pad_maximum_fusion.18.refs_6_), channel_id=1, source_target_pairs={{0,1},{16,17},{48,49},{32,33},{4,5},{20,21},{52,53},{36,37},{8,9},... | collective-permute-start | bytes 36872 | tf_op jit(solution)/shard_map/ppermute | solution.py:78
  209.2 5.0 %collective-permute-start.40 = (f32[3,8,128]{2,1,0:T(8,128)S(1)}, f32[3,8,128]{2,1,0:T(8,128)S(1)}, u32[]{:S(2)}, u32[]{:S(2)}) collective-permute-start(f32[3,8,128]{2,1,0:T(8,128)S(1)} %pad_maximum_fusion.20.refs_6_), channel_id=1, source_target_pairs={{0,1},{16,17},{48,49},{32,33},{4,5},{20,21},{52,53},{36,37},{8,9},... | collective-permute-start | bytes 36872 | tf_op jit(solution)/shard_map/ppermute | solution.py:78
  231.3 6.4 %collective-permute-start.44 = (f32[3,8,128]{2,1,0:T(8,128)S(1)}, f32[3,8,128]{2,1,0:T(8,128)S(1)}, u32[]{:S(2)}, u32[]{:S(2)}) collective-permute-start(f32[3,8,128]{2,1,0:T(8,128)S(1)} %pad_maximum_fusion.22.refs_6_), channel_id=1, source_target_pairs={{0,1},{16,17},{48,49},{32,33},{4,5},{20,21},{52,53},{36,37},{8,9},... | collective-permute-start | bytes 36872 | tf_op jit(solution)/shard_map/ppermute | solution.py:78
  245.8 4.5 %collective-permute-start.47 = (f32[4,8,128]{2,1,0:T(8,128)S(1)}, f32[4,8,128]{2,1,0:T(8,128)S(1)}, u32[]{:S(2)}, u32[]{:S(2)}) collective-permute-start(f32[4,8,128]{2,1,0:T(8,128)S(1)} %pad_maximum_fusion.3), channel_id=1, source_target_pairs={{16,48},{48,16},{32,4},{4,32},{20,52},{52,20},{36,8},{8,36},{24,56... | collective-permute-start | bytes 49160 | tf_op jit(solution)/shard_map/ppermute | solution.py:78
  252.7 6.6 %collective-permute-start.48 = (f32[4,8,128]{2,1,0:T(8,128)S(1)}, f32[4,8,128]{2,1,0:T(8,128)S(1)}, u32[]{:S(2)}, u32[]{:S(2)}) collective-permute-start(f32[4,8,128]{2,1,0:T(8,128)S(1)} %pad_maximum_fusion.4), channel_id=1, source_target_pairs={{0,1},{16,17},{48,49},{32,33},{4,5},{20,21},{52,53},{36,37},{8,9},... | collective-permute-start | bytes 49160 | tf_op jit(solution)/shard_map/ppermute | solution.py:78
  261.2 14.8 %collective-permute-start.50 = (f32[13,128]{1,0:T(8,128)S(1)}, f32[13,128]{1,0:T(8,128)S(1)}, u32[]{:S(2)}, u32[]{:S(2)}) collective-permute-start(f32[13,128]{1,0:T(8,128)S(1)} %bitcast.91), channel_id=1, source_target_pairs={{0,0},{16,1},{48,2},{32,3},{4,4},{20,5},{52,6},{36,7},{8,8},{24,9}... | collective-permute-start | bytes 19976 | tf_op jit(solution)/shard_map/ppermute | solution.py:78
  276.1 14.9 %collective-permute-start.51 = (f32[13,128]{1,0:T(8,128)S(1)}, f32[13,128]{1,0:T(8,128)S(1)}, u32[]{:S(2)}, u32[]{:S(2)}) collective-permute-start(f32[13,128]{1,0:T(8,128)S(1)} %bitcast.94), channel_id=1, source_target_pairs={{1,0},{17,1},{49,2},{33,3},{5,4},{21,5},{53,6},{37,7},{9,8},{25,9}... | collective-permute-start | bytes 19976 | tf_op jit(solution)/shard_map/ppermute | solution.py:78
  291.0 8.4 %collective-permute-start.52 = (f32[13,128]{1,0:T(8,128)S(1)}, f32[13,128]{1,0:T(8,128)S(1)}, u32[]{:S(2)}, u32[]{:S(2)}) collective-permute-start(f32[13,128]{1,0:T(8,128)S(1)} %bitcast.93), channel_id=1, source_target_pairs={{2,0},{18,1},{50,2},{34,3},{6,4},{22,5},{54,6},{38,7},{10,8},{26,9... | collective-permute-start | bytes 19976 | tf_op jit(solution)/shard_map/ppermute | solution.py:78
  304.2 5.1 %collective-permute-done.53 = f32[13,128]{1,0:T(8,128)S(1)} collective-permute-done((f32[13,128]{1,0:T(8,128)S(1)}, f32[13,128]{1,0:T(8,128)S(1)}, u32[]{:S(2)}, u32[]{:S(2)}) %collective-permute-start.53) | collective-permute-done | bytes 6688 | tf_op jit(solution)/shard_map/ppermute | solution.py:78
  (236 shorter events, 161.5 us)
Async XLA Ops:
  6.6 16.2 %collective-permute-start.2 = (f32[18,128]{1,0:T(8,128)S(1)}, f32[18,128]{1,0:T(8,128)S(1)}, u32[]{:S(2)}, u32[]{:S(2)}) collective-permute-start(f32[18,128]{1,0:T(8,128)S(1)} %get-tuple-element.141), channel_id=1, source_target_pairs={{0,1},{1,17},{2,49},{3,33},{4,5},{5,21},{6,53},{7,37},{8,9},{9,25}... | collective-permute-start | bytes 27656 | tf_op jit(solution)/shard_map/ppermute | solution.py:78
  12.2 10.6 %collective-permute-start.1 = (f32[18,128]{1,0:T(8,128)S(1)}, f32[18,128]{1,0:T(8,128)S(1)}, u32[]{:S(2)}, u32[]{:S(2)}) collective-permute-start(f32[18,128]{1,0:T(8,128)S(1)} %get-tuple-element.142), channel_id=1, source_target_pairs={{0,2},{1,18},{2,50},{3,34},{4,6},{5,22},{6,54},{7,38},{8,10},{9,26... | collective-permute-start | bytes 27656 | tf_op jit(solution)/shard_map/ppermute | solution.py:78
  20.7 7.7 %collective-permute-start.3 = (f32[18,128]{1,0:T(8,128)S(1)}, f32[18,128]{1,0:T(8,128)S(1)}, u32[]{:S(2)}, u32[]{:S(2)}) collective-permute-start(f32[18,128]{1,0:T(8,128)S(1)} %get-tuple-element.140), channel_id=1, source_target_pairs={{0,0},{1,16},{2,48},{3,32},{4,4},{5,20},{6,52},{7,36},{8,8},{9,24}... | collective-permute-start | bytes 27656 | tf_op jit(solution)/shard_map/ppermute | solution.py:78
  28.6 7.0 %collective-permute-start.4 = (f32[17,4,128]{2,1,0:T(4,128)S(1)}, f32[17,4,128]{2,1,0:T(4,128)S(1)}, u32[]{:S(2)}, u32[]{:S(2)}) collective-permute-start(f32[17,4,128]{2,1,0:T(4,128)S(1)} %slice.278), channel_id=1, source_target_pairs={{16,0},{48,16},{32,48},{4,32},{20,4},{52,20},{36,52},{8,36},{24,8}... | collective-permute-start | bytes 104456 | tf_op jit(solution)/shard_map/ppermute | solution.py:78
  51.2 6.8 %collective-permute-start.7 = (f32[3,8,128]{2,1,0:T(8,128)S(1)}, f32[3,8,128]{2,1,0:T(8,128)S(1)}, u32[]{:S(2)}, u32[]{:S(2)}) collective-permute-start(f32[3,8,128]{2,1,0:T(8,128)S(1)} %get-tuple-element.66), channel_id=1, source_target_pairs={{16,48},{48,16},{32,4},{4,32},{20,52},{52,20},{36,8},{8,36},{24,56... | collective-permute-start | bytes 36872 | tf_op jit(solution)/shard_map/ppermute | solution.py:78
  66.1 7.7 %collective-permute-start.11 = (f32[3,8,128]{2,1,0:T(8,128)S(1)}, f32[3,8,128]{2,1,0:T(8,128)S(1)}, u32[]{:S(2)}, u32[]{:S(2)}) collective-permute-start(f32[3,8,128]{2,1,0:T(8,128)S(1)} %get-tuple-element.70), channel_id=1, source_target_pairs={{16,48},{48,16},{32,4},{4,32},{20,52},{52,20},{36,8},{8,36},{24,56... | collective-permute-start | bytes 36872 | tf_op jit(solution)/shard_map/ppermute | solution.py:78
  83.0 7.3 %collective-permute-start.15 = (f32[3,8,128]{2,1,0:T(8,128)S(1)}, f32[3,8,128]{2,1,0:T(8,128)S(1)}, u32[]{:S(2)}, u32[]{:S(2)}) collective-permute-start(f32[3,8,128]{2,1,0:T(8,128)S(1)} %get-tuple-element.74), channel_id=1, source_target_pairs={{16,48},{48,16},{32,4},{4,32},{20,52},{52,20},{36,8},{8,36},{24,56... | collective-permute-start | bytes 36872 | tf_op jit(solution)/shard_map/ppermute | solution.py:78
  100.6 6.8 %collective-permute-start.19 = (f32[3,8,128]{2,1,0:T(8,128)S(1)}, f32[3,8,128]{2,1,0:T(8,128)S(1)}, u32[]{:S(2)}, u32[]{:S(2)}) collective-permute-start(f32[3,8,128]{2,1,0:T(8,128)S(1)} %get-tuple-element.78), channel_id=1, source_target_pairs={{16,48},{48,16},{32,4},{4,32},{20,52},{52,20},{36,8},{8,36},{24,56... | collective-permute-start | bytes 36872 | tf_op jit(solution)/shard_map/ppermute | solution.py:78
  107.4 7.2 %collective-permute-start.20 = (f32[3,8,128]{2,1,0:T(8,128)S(1)}, f32[3,8,128]{2,1,0:T(8,128)S(1)}, u32[]{:S(2)}, u32[]{:S(2)}) collective-permute-start(f32[3,8,128]{2,1,0:T(8,128)S(1)} %pad_maximum_fusion.12.refs_4_), channel_id=1, source_target_pairs={{0,1},{16,17},{48,49},{32,33},{4,5},{20,21},{52,53},{36,37},{8,9},... | collective-permute-start | bytes 36872 | tf_op jit(solution)/shard_map/ppermute | solution.py:78
  119.2 6.8 %collective-permute-start.23 = (f32[3,8,128]{2,1,0:T(8,128)S(1)}, f32[3,8,128]{2,1,0:T(8,128)S(1)}, u32[]{:S(2)}, u32[]{:S(2)}) collective-permute-start(f32[3,8,128]{2,1,0:T(8,128)S(1)} %get-tuple-element.82), channel_id=1, source_target_pairs={{16,48},{48,16},{32,4},{4,32},{20,52},{52,20},{36,8},{8,36},{24,56... | collective-permute-start | bytes 36872 | tf_op jit(solution)/shard_map/ppermute | solution.py:78
  138.6 6.9 %collective-permute-start.27 = (f32[6,8,128]{2,1,0:T(8,128)S(1)}, f32[6,8,128]{2,1,0:T(8,128)S(1)}, u32[]{:S(2)}, u32[]{:S(2)}) collective-permute-start(f32[6,8,128]{2,1,0:T(8,128)S(1)} %get-tuple-element.86), channel_id=1, source_target_pairs={{16,48},{48,16},{32,4},{4,32},{20,52},{52,20},{36,8},{8,36},{24,56... | collective-permute-start | bytes 73736 | tf_op jit(solution)/shard_map/ppermute | solution.py:78
  145.5 8.7 %collective-permute-start.28 = (f32[6,8,128]{2,1,0:T(8,128)S(1)}, f32[6,8,128]{2,1,0:T(8,128)S(1)}, u32[]{:S(2)}, u32[]{:S(2)}) collective-permute-start(f32[6,8,128]{2,1,0:T(8,128)S(1)} %pad_maximum_fusion.refs_6_), channel_id=1, source_target_pairs={{0,1},{16,17},{48,49},{32,33},{4,5},{20,21},{52,53},{36,37},{8,9},... | collective-permute-start | bytes 73736 | tf_op jit(solution)/shard_map/ppermute | solution.py:78
  160.7 6.8 %collective-permute-start.31 = (f32[3,8,128]{2,1,0:T(8,128)S(1)}, f32[3,8,128]{2,1,0:T(8,128)S(1)}, u32[]{:S(2)}, u32[]{:S(2)}) collective-permute-start(f32[3,8,128]{2,1,0:T(8,128)S(1)} %get-tuple-element.97), channel_id=1, source_target_pairs={{16,48},{48,16},{32,4},{4,32},{20,52},{52,20},{36,8},{8,36},{24,56... | collective-permute-start | bytes 36872 | tf_op jit(solution)/shard_map/ppermute | solution.py:78
  181.1 6.8 %collective-permute-start.35 = (f32[3,8,128]{2,1,0:T(8,128)S(1)}, f32[3,8,128]{2,1,0:T(8,128)S(1)}, u32[]{:S(2)}, u32[]{:S(2)}) collective-permute-start(f32[3,8,128]{2,1,0:T(8,128)S(1)} %get-tuple-element.102), channel_id=1, source_target_pairs={{16,48},{48,16},{32,4},{4,32},{20,52},{52,20},{36,8},{8,36},{24,56... | collective-permute-start | bytes 36872 | tf_op jit(solution)/shard_map/ppermute | solution.py:78
  187.9 7.0 %collective-permute-start.36 = (f32[3,8,128]{2,1,0:T(8,128)S(1)}, f32[3,8,128]{2,1,0:T(8,128)S(1)}, u32[]{:S(2)}, u32[]{:S(2)}) collective-permute-start(f32[3,8,128]{2,1,0:T(8,128)S(1)} %pad_maximum_fusion.18.refs_6_), channel_id=1, source_target_pairs={{0,1},{16,17},{48,49},{32,33},{4,5},{20,21},{52,53},{36,37},{8,9},... | collective-permute-start | bytes 36872 | tf_op jit(solution)/shard_map/ppermute | solution.py:78
  221.2 7.0 %collective-permute-start.42 = (f32[3,8,128]{2,1,0:T(8,128)S(1)}, f32[3,8,128]{2,1,0:T(8,128)S(1)}, u32[]{:S(2)}, u32[]{:S(2)}) collective-permute-start(f32[3,8,128]{2,1,0:T(8,128)S(1)} %get-tuple-element.111), channel_id=1, source_target_pairs={{0,16},{16,0},{48,32},{32,48},{4,20},{20,4},{52,36},{36,52},{8,24}... | collective-permute-start | bytes 36872 | tf_op jit(solution)/shard_map/ppermute | solution.py:78
  231.3 8.1 %collective-permute-start.44 = (f32[3,8,128]{2,1,0:T(8,128)S(1)}, f32[3,8,128]{2,1,0:T(8,128)S(1)}, u32[]{:S(2)}, u32[]{:S(2)}) collective-permute-start(f32[3,8,128]{2,1,0:T(8,128)S(1)} %pad_maximum_fusion.22.refs_6_), channel_id=1, source_target_pairs={{0,1},{16,17},{48,49},{32,33},{4,5},{20,21},{52,53},{36,37},{8,9},... | collective-permute-start | bytes 36872 | tf_op jit(solution)/shard_map/ppermute | solution.py:78
  243.3 7.1 %collective-permute-start.46 = (f32[4,8,128]{2,1,0:T(8,128)S(1)}, f32[4,8,128]{2,1,0:T(8,128)S(1)}, u32[]{:S(2)}, u32[]{:S(2)}) collective-permute-start(f32[4,8,128]{2,1,0:T(8,128)S(1)} %pad_maximum_fusion.2), channel_id=1, source_target_pairs={{0,16},{16,0},{48,32},{32,48},{4,20},{20,4},{52,36},{36,52},{8,24}... | collective-permute-start | bytes 49160 | tf_op jit(solution)/shard_map/ppermute | solution.py:78
  245.8 6.8 %collective-permute-start.47 = (f32[4,8,128]{2,1,0:T(8,128)S(1)}, f32[4,8,128]{2,1,0:T(8,128)S(1)}, u32[]{:S(2)}, u32[]{:S(2)}) collective-permute-start(f32[4,8,128]{2,1,0:T(8,128)S(1)} %pad_maximum_fusion.3), channel_id=1, source_target_pairs={{16,48},{48,16},{32,4},{4,32},{20,52},{52,20},{36,8},{8,36},{24,56... | collective-permute-start | bytes 49160 | tf_op jit(solution)/shard_map/ppermute | solution.py:78
  252.7 8.3 %collective-permute-start.48 = (f32[4,8,128]{2,1,0:T(8,128)S(1)}, f32[4,8,128]{2,1,0:T(8,128)S(1)}, u32[]{:S(2)}, u32[]{:S(2)}) collective-permute-start(f32[4,8,128]{2,1,0:T(8,128)S(1)} %pad_maximum_fusion.4), channel_id=1, source_target_pairs={{0,1},{16,17},{48,49},{32,33},{4,5},{20,21},{52,53},{36,37},{8,9},... | collective-permute-start | bytes 49160 | tf_op jit(solution)/shard_map/ppermute | solution.py:78
  261.2 41.4 %collective-permute-start.50 = (f32[13,128]{1,0:T(8,128)S(1)}, f32[13,128]{1,0:T(8,128)S(1)}, u32[]{:S(2)}, u32[]{:S(2)}) collective-permute-start(f32[13,128]{1,0:T(8,128)S(1)} %bitcast.91), channel_id=1, source_target_pairs={{0,0},{16,1},{48,2},{32,3},{4,4},{20,5},{52,6},{36,7},{8,8},{24,9}... | collective-permute-start | bytes 19976 | tf_op jit(solution)/shard_map/ppermute | solution.py:78
  276.1 26.5 %collective-permute-start.51 = (f32[13,128]{1,0:T(8,128)S(1)}, f32[13,128]{1,0:T(8,128)S(1)}, u32[]{:S(2)}, u32[]{:S(2)}) collective-permute-start(f32[13,128]{1,0:T(8,128)S(1)} %bitcast.94), channel_id=1, source_target_pairs={{1,0},{17,1},{49,2},{33,3},{5,4},{21,5},{53,6},{37,7},{9,8},{25,9}... | collective-permute-start | bytes 19976 | tf_op jit(solution)/shard_map/ppermute | solution.py:78
  291.0 13.1 %collective-permute-start.52 = (f32[13,128]{1,0:T(8,128)S(1)}, f32[13,128]{1,0:T(8,128)S(1)}, u32[]{:S(2)}, u32[]{:S(2)}) collective-permute-start(f32[13,128]{1,0:T(8,128)S(1)} %bitcast.93), channel_id=1, source_target_pairs={{2,0},{18,1},{50,2},{34,3},{6,4},{22,5},{54,6},{38,7},{10,8},{26,9... | collective-permute-start | bytes 19976 | tf_op jit(solution)/shard_map/ppermute | solution.py:78
  299.4 9.8 %collective-permute-start.53 = (f32[13,128]{1,0:T(8,128)S(1)}, f32[13,128]{1,0:T(8,128)S(1)}, u32[]{:S(2)}, u32[]{:S(2)}) collective-permute-start(f32[13,128]{1,0:T(8,128)S(1)} %bitcast.92), channel_id=1, source_target_pairs={{3,0},{19,1},{51,2},{35,3},{7,4},{23,5},{55,6},{39,7},{11,8},{27,9... | collective-permute-start | bytes 19976 | tf_op jit(solution)/shard_map/ppermute | solution.py:78
  (37 other events, 240.4 us)
where the time goes:
time: 312 us
  starting transfers between devices  179 us (57%)
  waiting for transfers between devices  71.2 us (23%)
  Pallas kernels  44.6 us (14%)
  local copies, waits for them, and re-layouts  9.09 us (3%)
  other arithmetic  5.81 us (2%)
    ppermute x54, starting transfers between devices, send(): return lax.ppermute(value, AXES, pairs)  179 us
    ppermute x54, waiting for transfers between devices, send(): return lax.ppermute(value, AXES, pairs)  71.2 us
    pallas_call x11, Pallas kernels, sweep(): pl.pallas_call(functools.partial(sweep_kernel, mode, first, kick), out_sh...  40.8 us
    unnamed x32, local copies, waits for them, and re-layouts  6.34 us
  transfers between devices with their start and end apart: 54, of which 28 were waited for; matrix products, arithmetic and copies ran while one was open for 0% of the time, Pallas kernels for 0%

commit v1 on v0

--- a/solution.py
+++ b/solution.py
@@ -21,7 +21,7 @@
 ROWS = 18
 TILES = 2
 GROUP = 8 * TILES
-JOBS = 6
+JOBS = 8
 LIST = 56 * (128 // GROUP) + 16
 
 

time: 312 us -> 301 us (0.965); the launches traced: 312 us -> 297 us
  waiting for transfers between devices: 71.2 us -> 55.5 us
  starting transfers between devices: 179 us -> 192 us
  Pallas kernels: 44.6 us -> 32 us
    ppermute x54, waiting for transfers between devices: 71.2 us -> 55.5 us  [send(): return lax.ppermute(value, AXES, pairs)]
    ppermute x54, starting transfers between devices: 179 us -> 192 us  [send(): return lax.ppermute(value, AXES, pairs)]
    pallas_call x11, Pallas kernels: 40.8 us -> 29.5 us  [sweep(): pl.pallas_call(functools.partial(sweep_kernel, mode, first, kick), out_sh...]
  transfers between devices with their start and end apart: 54 -> 54, of which waited for: 28 -> 28; matrix products, arithmetic and copies ran while one was open for 0% -> 1% of each run, Pallas kernels for 0% -> 0%
where the time goes in v1:
time: 301 us; the launch traced here: 297 us
  starting transfers between devices  192 us (64%)
  waiting for transfers between devices  55.5 us (18%)
  Pallas kernels  32 us (11%)
  local copies, waits for them, and re-layouts  9.09 us (3%)
  other arithmetic  5.81 us (2%)
    ppermute x54, starting transfers between devices, send(): return lax.ppermute(value, AXES, pairs)  192 us
    ppermute x54, waiting for transfers between devices, send(): return lax.ppermute(value, AXES, pairs)  55.5 us
    pallas_call x11, Pallas kernels, sweep(): pl.pallas_call(functools.partial(sweep_kernel, mode, first, kick), out_sh...  29.5 us
    unnamed x32, local copies, waits for them, and re-layouts  6.34 us
  transfers between devices with their start and end apart: 54, of which 28 were waited for; matrix products, arithmetic and copies ran while one was open for 1% of the time, Pallas kernels for 0%

profile of v1, /device:TPU:96, one launch (start us, length us, event | category | flops | bytes accessed | tf_op | source)
XLA Modules:
  0.0 297.3 jit_solution(5698202682978422413)
XLA Ops:
  6.6 5.6 %collective-permute-start.2 = (f32[18,128]{1,0:T(8,128)S(1)}, f32[18,128]{1,0:T(8,128)S(1)}, u32[]{:S(2)}, u32[]{:S(2)}) collective-permute-start(f32[18,128]{1,0:T(8,128)S(1)} %get-tuple-element.141), channel_id=1, source_target_pairs={{0,1},{1,17},{2,49},{3,33},{4,5},{5,21},{6,53},{7,37},{8,9},{9,25}... | collective-permute-start | bytes 27656 | tf_op jit(solution)/shard_map/ppermute | solution.py:78
  12.2 5.2 %collective-permute-start.1 = (f32[18,128]{1,0:T(8,128)S(1)}, f32[18,128]{1,0:T(8,128)S(1)}, u32[]{:S(2)}, u32[]{:S(2)}) collective-permute-start(f32[18,128]{1,0:T(8,128)S(1)} %get-tuple-element.142), channel_id=1, source_target_pairs={{0,2},{1,18},{2,50},{3,34},{4,6},{5,22},{6,54},{7,38},{8,10},{9,26... | collective-permute-start | bytes 27656 | tf_op jit(solution)/shard_map/ppermute | solution.py:78
  31.1 4.5 %collective-permute-done.4 = f32[17,4,128]{2,1,0:T(4,128)S(1)} collective-permute-done((f32[17,4,128]{2,1,0:T(4,128)S(1)}, f32[17,4,128]{2,1,0:T(4,128)S(1)}, u32[]{:S(2)}, u32[]{:S(2)}) %collective-permute-start.4) | collective-permute-done | bytes 34848 | tf_op jit(solution)/shard_map/ppermute | solution.py:78
  49.2 5.4 %collective-permute-start.7 = (f32[3,8,128]{2,1,0:T(8,128)S(1)}, f32[3,8,128]{2,1,0:T(8,128)S(1)}, u32[]{:S(2)}, u32[]{:S(2)}) collective-permute-start(f32[3,8,128]{2,1,0:T(8,128)S(1)} %get-tuple-element.66), channel_id=1, source_target_pairs={{16,48},{48,16},{32,4},{4,32},{20,52},{52,20},{36,8},{8,36},{24,56... | collective-permute-start | bytes 36872 | tf_op jit(solution)/shard_map/ppermute | solution.py:78
  63.9 6.2 %collective-permute-start.11 = (f32[3,8,128]{2,1,0:T(8,128)S(1)}, f32[3,8,128]{2,1,0:T(8,128)S(1)}, u32[]{:S(2)}, u32[]{:S(2)}) collective-permute-start(f32[3,8,128]{2,1,0:T(8,128)S(1)} %get-tuple-element.70), channel_id=1, source_target_pairs={{16,48},{48,16},{32,4},{4,32},{20,52},{52,20},{36,8},{8,36},{24,56... | collective-permute-start | bytes 36872 | tf_op jit(solution)/shard_map/ppermute | solution.py:78
  81.1 7.6 %collective-permute-start.15 = (f32[3,8,128]{2,1,0:T(8,128)S(1)}, f32[3,8,128]{2,1,0:T(8,128)S(1)}, u32[]{:S(2)}, u32[]{:S(2)}) collective-permute-start(f32[3,8,128]{2,1,0:T(8,128)S(1)} %get-tuple-element.74), channel_id=1, source_target_pairs={{16,48},{48,16},{32,4},{4,32},{20,52},{52,20},{36,8},{8,36},{24,56... | collective-permute-start | bytes 36872 | tf_op jit(solution)/shard_map/ppermute | solution.py:78
  90.4 5.1 %collective-permute-start.16 = (f32[3,8,128]{2,1,0:T(8,128)S(1)}, f32[3,8,128]{2,1,0:T(8,128)S(1)}, u32[]{:S(2)}, u32[]{:S(2)}) collective-permute-start(f32[3,8,128]{2,1,0:T(8,128)S(1)} %pad_maximum_fusion.10.refs_4_), channel_id=1, source_target_pairs={{0,1},{16,17},{48,49},{32,33},{4,5},{20,21},{52,53},{36,37},{8,9},... | collective-permute-start | bytes 36872 | tf_op jit(solution)/shard_map/ppermute | solution.py:78
  99.8 6.8 %collective-permute-start.19 = (f32[3,8,128]{2,1,0:T(8,128)S(1)}, f32[3,8,128]{2,1,0:T(8,128)S(1)}, u32[]{:S(2)}, u32[]{:S(2)}) collective-permute-start(f32[3,8,128]{2,1,0:T(8,128)S(1)} %get-tuple-element.78), channel_id=1, source_target_pairs={{16,48},{48,16},{32,4},{4,32},{20,52},{52,20},{36,8},{8,36},{24,56... | collective-permute-start | bytes 36872 | tf_op jit(solution)/shard_map/ppermute | solution.py:78
  108.3 8.9 %collective-permute-start.20 = (f32[3,8,128]{2,1,0:T(8,128)S(1)}, f32[3,8,128]{2,1,0:T(8,128)S(1)}, u32[]{:S(2)}, u32[]{:S(2)}) collective-permute-start(f32[3,8,128]{2,1,0:T(8,128)S(1)} %pad_maximum_fusion.12.refs_4_), channel_id=1, source_target_pairs={{0,1},{16,17},{48,49},{32,33},{4,5},{20,21},{52,53},{36,37},{8,9},... | collective-permute-start | bytes 36872 | tf_op jit(solution)/shard_map/ppermute | solution.py:78
  121.3 6.6 %collective-permute-start.23 = (f32[3,8,128]{2,1,0:T(8,128)S(1)}, f32[3,8,128]{2,1,0:T(8,128)S(1)}, u32[]{:S(2)}, u32[]{:S(2)}) collective-permute-start(f32[3,8,128]{2,1,0:T(8,128)S(1)} %get-tuple-element.82), channel_id=1, source_target_pairs={{16,48},{48,16},{32,4},{4,32},{20,52},{52,20},{36,8},{8,36},{24,56... | collective-permute-start | bytes 36872 | tf_op jit(solution)/shard_map/ppermute | solution.py:78
  129.5 5.5 %collective-permute-start.24 = (f32[3,8,128]{2,1,0:T(8,128)S(1)}, f32[3,8,128]{2,1,0:T(8,128)S(1)}, u32[]{:S(2)}, u32[]{:S(2)}) collective-permute-start(f32[3,8,128]{2,1,0:T(8,128)S(1)} %pad_maximum_fusion.14.refs_4_), channel_id=1, source_target_pairs={{0,1},{16,17},{48,49},{32,33},{4,5},{20,21},{52,53},{36,37},{8,9},... | collective-permute-start | bytes 36872 | tf_op jit(solution)/shard_map/ppermute | solution.py:78
  140.6 7.6 %collective-permute-start.27 = (f32[6,8,128]{2,1,0:T(8,128)S(1)}, f32[6,8,128]{2,1,0:T(8,128)S(1)}, u32[]{:S(2)}, u32[]{:S(2)}) collective-permute-start(f32[6,8,128]{2,1,0:T(8,128)S(1)} %get-tuple-element.86), channel_id=1, source_target_pairs={{16,48},{48,16},{32,4},{4,32},{20,52},{52,20},{36,8},{8,36},{24,56... | collective-permute-start | bytes 73736 | tf_op jit(solution)/shard_map/ppermute | solution.py:78
  150.1 7.0 %collective-permute-start.28 = (f32[6,8,128]{2,1,0:T(8,128)S(1)}, f32[6,8,128]{2,1,0:T(8,128)S(1)}, u32[]{:S(2)}, u32[]{:S(2)}) collective-permute-start(f32[6,8,128]{2,1,0:T(8,128)S(1)} %pad_maximum_fusion.refs_6_), channel_id=1, source_target_pairs={{0,1},{16,17},{48,49},{32,33},{4,5},{20,21},{52,53},{36,37},{8,9},... | collective-permute-start | bytes 73736 | tf_op jit(solution)/shard_map/ppermute | solution.py:78
  161.7 7.4 %collective-permute-start.31 = (f32[3,8,128]{2,1,0:T(8,128)S(1)}, f32[3,8,128]{2,1,0:T(8,128)S(1)}, u32[]{:S(2)}, u32[]{:S(2)}) collective-permute-start(f32[3,8,128]{2,1,0:T(8,128)S(1)} %get-tuple-element.97), channel_id=1, source_target_pairs={{16,48},{48,16},{32,4},{4,32},{20,52},{52,20},{36,8},{8,36},{24,56... | collective-permute-start | bytes 36872 | tf_op jit(solution)/shard_map/ppermute | solution.py:78
  170.8 5.9 %collective-permute-start.32 = (f32[3,8,128]{2,1,0:T(8,128)S(1)}, f32[3,8,128]{2,1,0:T(8,128)S(1)}, u32[]{:S(2)}, u32[]{:S(2)}) collective-permute-start(f32[3,8,128]{2,1,0:T(8,128)S(1)} %pad_maximum_fusion.16.refs_6_), channel_id=1, source_target_pairs={{0,1},{16,17},{48,49},{32,33},{4,5},{20,21},{52,53},{36,37},{8,9},... | collective-permute-start | bytes 36872 | tf_op jit(solution)/shard_map/ppermute | solution.py:78
  183.3 5.4 %collective-permute-start.35 = (f32[3,8,128]{2,1,0:T(8,128)S(1)}, f32[3,8,128]{2,1,0:T(8,128)S(1)}, u32[]{:S(2)}, u32[]{:S(2)}) collective-permute-start(f32[3,8,128]{2,1,0:T(8,128)S(1)} %get-tuple-element.102), channel_id=1, source_target_pairs={{16,48},{48,16},{32,4},{4,32},{20,52},{52,20},{36,8},{8,36},{24,56... | collective-permute-start | bytes 36872 | tf_op jit(solution)/shard_map/ppermute | solution.py:78
  190.4 7.5 %collective-permute-start.36 = (f32[3,8,128]{2,1,0:T(8,128)S(1)}, f32[3,8,128]{2,1,0:T(8,128)S(1)}, u32[]{:S(2)}, u32[]{:S(2)}) collective-permute-start(f32[3,8,128]{2,1,0:T(8,128)S(1)} %pad_maximum_fusion.18.refs_6_), channel_id=1, source_target_pairs={{0,1},{16,17},{48,49},{32,33},{4,5},{20,21},{52,53},{36,37},{8,9},... | collective-permute-start | bytes 36872 | tf_op jit(solution)/shard_map/ppermute | solution.py:78
  204.8 5.0 %collective-permute-start.39 = (f32[3,8,128]{2,1,0:T(8,128)S(1)}, f32[3,8,128]{2,1,0:T(8,128)S(1)}, u32[]{:S(2)}, u32[]{:S(2)}) collective-permute-start(f32[3,8,128]{2,1,0:T(8,128)S(1)} %get-tuple-element.107), channel_id=1, source_target_pairs={{16,48},{48,16},{32,4},{4,32},{20,52},{52,20},{36,8},{8,36},{24,56... | collective-permute-start | bytes 36872 | tf_op jit(solution)/shard_map/ppermute | solution.py:78
  211.7 6.3 %collective-permute-start.40 = (f32[3,8,128]{2,1,0:T(8,128)S(1)}, f32[3,8,128]{2,1,0:T(8,128)S(1)}, u32[]{:S(2)}, u32[]{:S(2)}) collective-permute-start(f32[3,8,128]{2,1,0:T(8,128)S(1)} %pad_maximum_fusion.20.refs_6_), channel_id=1, source_target_pairs={{0,1},{16,17},{48,49},{32,33},{4,5},{20,21},{52,53},{36,37},{8,9},... | collective-permute-start | bytes 36872 | tf_op jit(solution)/shard_map/ppermute | solution.py:78
  234.5 5.9 %collective-permute-start.44 = (f32[3,8,128]{2,1,0:T(8,128)S(1)}, f32[3,8,128]{2,1,0:T(8,128)S(1)}, u32[]{:S(2)}, u32[]{:S(2)}) collective-permute-start(f32[3,8,128]{2,1,0:T(8,128)S(1)} %pad_maximum_fusion.22.refs_6_), channel_id=1, source_target_pairs={{0,1},{16,17},{48,49},{32,33},{4,5},{20,21},{52,53},{36,37},{8,9},... | collective-permute-start | bytes 36872 | tf_op jit(solution)/shard_map/ppermute | solution.py:78
  244.8 4.5 %collective-permute-start.46 = (f32[4,8,128]{2,1,0:T(8,128)S(1)}, f32[4,8,128]{2,1,0:T(8,128)S(1)}, u32[]{:S(2)}, u32[]{:S(2)}) collective-permute-start(f32[4,8,128]{2,1,0:T(8,128)S(1)} %pad_maximum_fusion.2), channel_id=1, source_target_pairs={{0,16},{16,0},{48,32},{32,48},{4,20},{20,4},{52,36},{36,52},{8,24}... | collective-permute-start | bytes 49160 | tf_op jit(solution)/shard_map/ppermute | solution.py:78
  262.5 14.6 %collective-permute-start.50 = (f32[13,128]{1,0:T(8,128)S(1)}, f32[13,128]{1,0:T(8,128)S(1)}, u32[]{:S(2)}, u32[]{:S(2)}) collective-permute-start(f32[13,128]{1,0:T(8,128)S(1)} %bitcast.91), channel_id=1, source_target_pairs={{0,0},{16,1},{48,2},{32,3},{4,4},{20,5},{52,6},{36,7},{8,8},{24,9}... | collective-permute-start | bytes 19976 | tf_op jit(solution)/shard_map/ppermute | solution.py:78
  279.0 5.9 %collective-permute-start.52 = (f32[13,128]{1,0:T(8,128)S(1)}, f32[13,128]{1,0:T(8,128)S(1)}, u32[]{:S(2)}, u32[]{:S(2)}) collective-permute-start(f32[13,128]{1,0:T(8,128)S(1)} %bitcast.93), channel_id=1, source_target_pairs={{2,0},{18,1},{50,2},{34,3},{6,4},{22,5},{54,6},{38,7},{10,8},{26,9... | collective-permute-start | bytes 19976 | tf_op jit(solution)/shard_map/ppermute | solution.py:78
  289.4 4.8 %collective-permute-done.53 = f32[13,128]{1,0:T(8,128)S(1)} collective-permute-done((f32[13,128]{1,0:T(8,128)S(1)}, f32[13,128]{1,0:T(8,128)S(1)}, u32[]{:S(2)}, u32[]{:S(2)}) %collective-permute-start.53) | collective-permute-done | bytes 6688 | tf_op jit(solution)/shard_map/ppermute | solution.py:78
  (236 shorter events, 139.8 us)
Async XLA Ops:
  6.6 16.2 %collective-permute-start.2 = (f32[18,128]{1,0:T(8,128)S(1)}, f32[18,128]{1,0:T(8,128)S(1)}, u32[]{:S(2)}, u32[]{:S(2)}) collective-permute-start(f32[18,128]{1,0:T(8,128)S(1)} %get-tuple-element.141), channel_id=1, source_target_pairs={{0,1},{1,17},{2,49},{3,33},{4,5},{5,21},{6,53},{7,37},{8,9},{9,25}... | collective-permute-start | bytes 27656 | tf_op jit(solution)/shard_map/ppermute | solution.py:78
  12.2 10.6 %collective-permute-start.1 = (f32[18,128]{1,0:T(8,128)S(1)}, f32[18,128]{1,0:T(8,128)S(1)}, u32[]{:S(2)}, u32[]{:S(2)}) collective-permute-start(f32[18,128]{1,0:T(8,128)S(1)} %get-tuple-element.142), channel_id=1, source_target_pairs={{0,2},{1,18},{2,50},{3,34},{4,6},{5,22},{6,54},{7,38},{8,10},{9,26... | collective-permute-start | bytes 27656 | tf_op jit(solution)/shard_map/ppermute | solution.py:78
  20.7 7.7 %collective-permute-start.3 = (f32[18,128]{1,0:T(8,128)S(1)}, f32[18,128]{1,0:T(8,128)S(1)}, u32[]{:S(2)}, u32[]{:S(2)}) collective-permute-start(f32[18,128]{1,0:T(8,128)S(1)} %get-tuple-element.140), channel_id=1, source_target_pairs={{0,0},{1,16},{2,48},{3,32},{4,4},{5,20},{6,52},{7,36},{8,8},{9,24}... | collective-permute-start | bytes 27656 | tf_op jit(solution)/shard_map/ppermute | solution.py:78
  63.9 7.8 %collective-permute-start.11 = (f32[3,8,128]{2,1,0:T(8,128)S(1)}, f32[3,8,128]{2,1,0:T(8,128)S(1)}, u32[]{:S(2)}, u32[]{:S(2)}) collective-permute-start(f32[3,8,128]{2,1,0:T(8,128)S(1)} %get-tuple-element.70), channel_id=1, source_target_pairs={{16,48},{48,16},{32,4},{4,32},{20,52},{52,20},{36,8},{8,36},{24,56... | collective-permute-start | bytes 36872 | tf_op jit(solution)/shard_map/ppermute | solution.py:78
  79.7 9.0 %collective-permute-start.14 = (f32[3,8,128]{2,1,0:T(8,128)S(1)}, f32[3,8,128]{2,1,0:T(8,128)S(1)}, u32[]{:S(2)}, u32[]{:S(2)}) collective-permute-start(f32[3,8,128]{2,1,0:T(8,128)S(1)} %get-tuple-element.73), channel_id=1, source_target_pairs={{0,16},{16,0},{48,32},{32,48},{4,20},{20,4},{52,36},{36,52},{8,24}... | collective-permute-start | bytes 36872 | tf_op jit(solution)/shard_map/ppermute | solution.py:78
  81.1 9.3 %collective-permute-start.15 = (f32[3,8,128]{2,1,0:T(8,128)S(1)}, f32[3,8,128]{2,1,0:T(8,128)S(1)}, u32[]{:S(2)}, u32[]{:S(2)}) collective-permute-start(f32[3,8,128]{2,1,0:T(8,128)S(1)} %get-tuple-element.74), channel_id=1, source_target_pairs={{16,48},{48,16},{32,4},{4,32},{20,52},{52,20},{36,8},{8,36},{24,56... | collective-permute-start | bytes 36872 | tf_op jit(solution)/shard_map/ppermute | solution.py:78
  99.8 8.5 %collective-permute-start.19 = (f32[3,8,128]{2,1,0:T(8,128)S(1)}, f32[3,8,128]{2,1,0:T(8,128)S(1)}, u32[]{:S(2)}, u32[]{:S(2)}) collective-permute-start(f32[3,8,128]{2,1,0:T(8,128)S(1)} %get-tuple-element.78), channel_id=1, source_target_pairs={{16,48},{48,16},{32,4},{4,32},{20,52},{52,20},{36,8},{8,36},{24,56... | collective-permute-start | bytes 36872 | tf_op jit(solution)/shard_map/ppermute | solution.py:78
  108.3 10.6 %collective-permute-start.20 = (f32[3,8,128]{2,1,0:T(8,128)S(1)}, f32[3,8,128]{2,1,0:T(8,128)S(1)}, u32[]{:S(2)}, u32[]{:S(2)}) collective-permute-start(f32[3,8,128]{2,1,0:T(8,128)S(1)} %pad_maximum_fusion.12.refs_4_), channel_id=1, source_target_pairs={{0,1},{16,17},{48,49},{32,33},{4,5},{20,21},{52,53},{36,37},{8,9},... | collective-permute-start | bytes 36872 | tf_op jit(solution)/shard_map/ppermute | solution.py:78
  121.3 8.2 %collective-permute-start.23 = (f32[3,8,128]{2,1,0:T(8,128)S(1)}, f32[3,8,128]{2,1,0:T(8,128)S(1)}, u32[]{:S(2)}, u32[]{:S(2)}) collective-permute-start(f32[3,8,128]{2,1,0:T(8,128)S(1)} %get-tuple-element.82), channel_id=1, source_target_pairs={{16,48},{48,16},{32,4},{4,32},{20,52},{52,20},{36,8},{8,36},{24,56... | collective-permute-start | bytes 36872 | tf_op jit(solution)/shard_map/ppermute | solution.py:78
  140.5 7.7 %collective-permute-start.26 = (f32[6,8,128]{2,1,0:T(8,128)S(1)}, f32[6,8,128]{2,1,0:T(8,128)S(1)}, u32[]{:S(2)}, u32[]{:S(2)}) collective-permute-start(f32[6,8,128]{2,1,0:T(8,128)S(1)} %get-tuple-element.85), channel_id=1, source_target_pairs={{0,16},{16,0},{48,32},{32,48},{4,20},{20,4},{52,36},{36,52},{8,24}... | collective-permute-start | bytes 73736 | tf_op jit(solution)/shard_map/ppermute | solution.py:78
  140.6 9.4 %collective-permute-start.27 = (f32[6,8,128]{2,1,0:T(8,128)S(1)}, f32[6,8,128]{2,1,0:T(8,128)S(1)}, u32[]{:S(2)}, u32[]{:S(2)}) collective-permute-start(f32[6,8,128]{2,1,0:T(8,128)S(1)} %get-tuple-element.86), channel_id=1, source_target_pairs={{16,48},{48,16},{32,4},{4,32},{20,52},{52,20},{36,8},{8,36},{24,56... | collective-permute-start | bytes 73736 | tf_op jit(solution)/shard_map/ppermute | solution.py:78
  150.1 8.8 %collective-permute-start.28 = (f32[6,8,128]{2,1,0:T(8,128)S(1)}, f32[6,8,128]{2,1,0:T(8,128)S(1)}, u32[]{:S(2)}, u32[]{:S(2)}) collective-permute-start(f32[6,8,128]{2,1,0:T(8,128)S(1)} %pad_maximum_fusion.refs_6_), channel_id=1, source_target_pairs={{0,1},{16,17},{48,49},{32,33},{4,5},{20,21},{52,53},{36,37},{8,9},... | collective-permute-start | bytes 73736 | tf_op jit(solution)/shard_map/ppermute | solution.py:78
  161.6 7.5 %collective-permute-start.30 = (f32[3,8,128]{2,1,0:T(8,128)S(1)}, f32[3,8,128]{2,1,0:T(8,128)S(1)}, u32[]{:S(2)}, u32[]{:S(2)}) collective-permute-start(f32[3,8,128]{2,1,0:T(8,128)S(1)} %get-tuple-element.96), channel_id=1, source_target_pairs={{0,16},{16,0},{48,32},{32,48},{4,20},{20,4},{52,36},{36,52},{8,24}... | collective-permute-start | bytes 36872 | tf_op jit(solution)/shard_map/ppermute | solution.py:78
  161.7 9.0 %collective-permute-start.31 = (f32[3,8,128]{2,1,0:T(8,128)S(1)}, f32[3,8,128]{2,1,0:T(8,128)S(1)}, u32[]{:S(2)}, u32[]{:S(2)}) collective-permute-start(f32[3,8,128]{2,1,0:T(8,128)S(1)} %get-tuple-element.97), channel_id=1, source_target_pairs={{16,48},{48,16},{32,4},{4,32},{20,52},{52,20},{36,8},{8,36},{24,56... | collective-permute-start | bytes 36872 | tf_op jit(solution)/shard_map/ppermute | solution.py:78
  170.8 7.6 %collective-permute-start.32 = (f32[3,8,128]{2,1,0:T(8,128)S(1)}, f32[3,8,128]{2,1,0:T(8,128)S(1)}, u32[]{:S(2)}, u32[]{:S(2)}) collective-permute-start(f32[3,8,128]{2,1,0:T(8,128)S(1)} %pad_maximum_fusion.16.refs_6_), channel_id=1, source_target_pairs={{0,1},{16,17},{48,49},{32,33},{4,5},{20,21},{52,53},{36,37},{8,9},... | collective-permute-start | bytes 36872 | tf_op jit(solution)/shard_map/ppermute | solution.py:78
  190.4 9.2 %collective-permute-start.36 = (f32[3,8,128]{2,1,0:T(8,128)S(1)}, f32[3,8,128]{2,1,0:T(8,128)S(1)}, u32[]{:S(2)}, u32[]{:S(2)}) collective-permute-start(f32[3,8,128]{2,1,0:T(8,128)S(1)} %pad_maximum_fusion.18.refs_6_), channel_id=1, source_target_pairs={{0,1},{16,17},{48,49},{32,33},{4,5},{20,21},{52,53},{36,37},{8,9},... | collective-permute-start | bytes 36872 | tf_op jit(solution)/shard_map/ppermute | solution.py:78
  211.7 8.0 %collective-permute-start.40 = (f32[3,8,128]{2,1,0:T(8,128)S(1)}, f32[3,8,128]{2,1,0:T(8,128)S(1)}, u32[]{:S(2)}, u32[]{:S(2)}) collective-permute-start(f32[3,8,128]{2,1,0:T(8,128)S(1)} %pad_maximum_fusion.20.refs_6_), channel_id=1, source_target_pairs={{0,1},{16,17},{48,49},{32,33},{4,5},{20,21},{52,53},{36,37},{8,9},... | collective-permute-start | bytes 36872 | tf_op jit(solution)/shard_map/ppermute | solution.py:78
  223.8 7.5 %collective-permute-start.42 = (f32[3,8,128]{2,1,0:T(8,128)S(1)}, f32[3,8,128]{2,1,0:T(8,128)S(1)}, u32[]{:S(2)}, u32[]{:S(2)}) collective-permute-start(f32[3,8,128]{2,1,0:T(8,128)S(1)} %get-tuple-element.111), channel_id=1, source_target_pairs={{0,16},{16,0},{48,32},{32,48},{4,20},{20,4},{52,36},{36,52},{8,24}... | collective-permute-start | bytes 36872 | tf_op jit(solution)/shard_map/ppermute | solution.py:78
  234.5 7.6 %collective-permute-start.44 = (f32[3,8,128]{2,1,0:T(8,128)S(1)}, f32[3,8,128]{2,1,0:T(8,128)S(1)}, u32[]{:S(2)}, u32[]{:S(2)}) collective-permute-start(f32[3,8,128]{2,1,0:T(8,128)S(1)} %pad_maximum_fusion.22.refs_6_), channel_id=1, source_target_pairs={{0,1},{16,17},{48,49},{32,33},{4,5},{20,21},{52,53},{36,37},{8,9},... | collective-permute-start | bytes 36872 | tf_op jit(solution)/shard_map/ppermute | solution.py:78
  244.8 7.6 %collective-permute-start.46 = (f32[4,8,128]{2,1,0:T(8,128)S(1)}, f32[4,8,128]{2,1,0:T(8,128)S(1)}, u32[]{:S(2)}, u32[]{:S(2)}) collective-permute-start(f32[4,8,128]{2,1,0:T(8,128)S(1)} %pad_maximum_fusion.2), channel_id=1, source_target_pairs={{0,16},{16,0},{48,32},{32,48},{4,20},{20,4},{52,36},{36,52},{8,24}... | collective-permute-start | bytes 49160 | tf_op jit(solution)/shard_map/ppermute | solution.py:78
  262.5 25.0 %collective-permute-start.50 = (f32[13,128]{1,0:T(8,128)S(1)}, f32[13,128]{1,0:T(8,128)S(1)}, u32[]{:S(2)}, u32[]{:S(2)}) collective-permute-start(f32[13,128]{1,0:T(8,128)S(1)} %bitcast.91), channel_id=1, source_target_pairs={{0,0},{16,1},{48,2},{32,3},{4,4},{20,5},{52,6},{36,7},{8,8},{24,9}... | collective-permute-start | bytes 19976 | tf_op jit(solution)/shard_map/ppermute | solution.py:78
  277.1 10.4 %collective-permute-start.51 = (f32[13,128]{1,0:T(8,128)S(1)}, f32[13,128]{1,0:T(8,128)S(1)}, u32[]{:S(2)}, u32[]{:S(2)}) collective-permute-start(f32[13,128]{1,0:T(8,128)S(1)} %bitcast.94), channel_id=1, source_target_pairs={{1,0},{17,1},{49,2},{33,3},{5,4},{21,5},{53,6},{37,7},{9,8},{25,9}... | collective-permute-start | bytes 19976 | tf_op jit(solution)/shard_map/ppermute | solution.py:78
  279.0 10.4 %collective-permute-start.52 = (f32[13,128]{1,0:T(8,128)S(1)}, f32[13,128]{1,0:T(8,128)S(1)}, u32[]{:S(2)}, u32[]{:S(2)}) collective-permute-start(f32[13,128]{1,0:T(8,128)S(1)} %bitcast.93), channel_id=1, source_target_pairs={{2,0},{18,1},{50,2},{34,3},{6,4},{22,5},{54,6},{38,7},{10,8},{26,9... | collective-permute-start | bytes 19976 | tf_op jit(solution)/shard_map/ppermute | solution.py:78
  284.9 9.3 %collective-permute-start.53 = (f32[13,128]{1,0:T(8,128)S(1)}, f32[13,128]{1,0:T(8,128)S(1)}, u32[]{:S(2)}, u32[]{:S(2)}) collective-permute-start(f32[13,128]{1,0:T(8,128)S(1)} %bitcast.92), channel_id=1, source_target_pairs={{3,0},{19,1},{51,2},{35,3},{7,4},{23,5},{55,6},{39,7},{11,8},{27,9... | collective-permute-start | bytes 19976 | tf_op jit(solution)/shard_map/ppermute | solution.py:78
  (37 other events, 241.5 us)
